TPU v7x, 32 devices: a whole 2x2x4 slice. The times are simulated.
32 devices in a mesh: batch: 4 (over y, x), strip: 8 (over z, core).
Axes of the slice: x: 2, y: 2, z: 4, core: 2. Of those that a mesh axis runs over, the one named last changes fastest.
Arguments:
- camera_features: bfloat16 [4, 16896, 256], P('batch', 'strip'), may hold values from -6 to 6
- lidar_bev: bfloat16 [4, 48, 180, 256], P('batch', 'strip'), may hold values from -6 to 6
- pool_index: int32 [4, 16896, 118], P('batch', 'strip'), may hold values from 0 to 8639, as said below
- box_peaks: int32 [4, 3, 150], P('batch'), may hold values from 0 to 179, as said below
- box_count: int32 [4], P('batch'), may hold values from 1 to 150
- w_depth: float32 [256, 198], replicated, may hold values from -1 to 1
- m_depth: float32 [256, 198], replicated, may hold values from -7.6293945e-05 to 7.6293945e-05
- v_depth: float32 [256, 198], replicated, may hold values from 9.864268e-13 to 1.5782828e-11
- w_join: float32 [3, 3, 336, 256], P(None, None, None, 'strip'), may hold values from -0.109375 to 0.109375
- m_join: float32 [3, 3, 336, 256], P(None, None, None, 'strip'), may hold values from -1.9073486e-05 to 1.9073486e-05
- v_join: float32 [3, 3, 336, 256], P(None, None, None, 'strip'), may hold values from 6.458747e-14 to 1.0333995e-12
- w_res: float32 [3, 3, 256, 256], P(None, None, None, 'strip'), may hold values from -0.125 to 0.125
- m_res: float32 [3, 3, 256, 256], P(None, None, None, 'strip'), may hold values from -2.2888184e-05 to 2.2888184e-05
- v_res: float32 [3, 3, 256, 256], P(None, None, None, 'strip'), may hold values from 8.477105e-14 to 1.3563368e-12
- w_head: float32 [256, 10], replicated, may hold values from -0.375 to 0.375
- m_head: float32 [256, 10], replicated, may hold values from -0.00030517578 to 0.00030517578
- v_head: float32 [256, 10], replicated, may hold values from 1.953125e-11 to 3.125e-10
- norm_params: float32 [4, 256], replicated, may hold values from 0.25 to 1.75
- m_norm: float32 [4, 256], replicated, may hold values from -0.00048828125 to 0.00048828125
- v_norm: float32 [4, 256], replicated, may hold values from 4.8828126e-11 to 7.8125e-10
- head_bias: float32 [10], replicated, may hold values from -2.5 to -1.5
- m_bias: float32 [10], replicated, may hold values from -0.0048828125 to 0.0048828125
- v_bias: float32 [10], replicated, may hold values from 5e-09 to 8e-08
Outputs:
- loss: float32 [1], replicated
- grad_norms: float32 [6], replicated
- new_w_depth: float32 [256, 198], replicated
- new_m_depth: float32 [256, 198], replicated
- new_v_depth: float32 [256, 198], replicated
- new_w_join: float32 [3, 3, 336, 256], P(None, None, None, 'strip')
- new_m_join: float32 [3, 3, 336, 256], P(None, None, None, 'strip')
- new_v_join: float32 [3, 3, 336, 256], P(None, None, None, 'strip')
- new_w_res: float32 [3, 3, 256, 256], P(None, None, None, 'strip')
- new_m_res: float32 [3, 3, 256, 256], P(None, None, None, 'strip')
- new_v_res: float32 [3, 3, 256, 256], P(None, None, None, 'strip')
- new_w_head: float32 [256, 10], replicated
- new_m_head: float32 [256, 10], replicated
- new_v_head: float32 [256, 10], replicated
- new_norm: float32 [4, 256], replicated
- new_m_norm: float32 [4, 256], replicated
- new_v_norm: float32 [4, 256], replicated
- new_bias: float32 [10], replicated
- new_m_bias: float32 [10], replicated
- new_v_bias: float32 [10], replicated
Inputs may be any that keep to these rules, and one draw needn't show every extreme that they name: `pool_index`: cell = row * 180 + column of one sample's grid; rows near the middle of the grid are named more often. `box_peaks`: per slot: row below 48, column below 180, class below 10.
All inputs are finite; a program needn't handle non-finite values.
Results may differ from a plain program's by a relative error of at most 0.015.
Values may be sent and summed in bfloat16 or wider, within the bound.
No kernel may reach another device: no remote copies, remote signals or barrier semaphores. Data moves between devices by JAX's collectives and lax.ppermute only.
A program may use at most 192 MiB of HBM per device.

v0:
```python
import jax
import jax.numpy as jnp
from jax import lax
from jax.sharding import PartitionSpec as P

STEP = 5


EPS_NORM = 1e-05
SPREAD_TWICE = 8.0
SMALL_RATE = 0.25
CLIP_NORM = 0.01
pixel_block = 512


def extended(shard, sides, width):
    for axis, dim in sides:
        peers, length = (lax.axis_size(axis), shard.shape[dim])
        up = [(i, (i + 1) % peers) for i in range(peers - 1)]
        down = [(j, i) for i, j in up]
        last = lax.slice_in_dim(shard, length - width, length, axis=dim)
        leading = lax.slice_in_dim(shard, 0, width, axis=dim)
        before = lax.ppermute(last, axis, up)
        after = lax.ppermute(leading, axis, down)
        shard = jnp.concatenate([before, shard, after], axis=dim)
    return shard


def targets(box_peaks, box_count, first_row, row_total, col_total, classes):
    row_ids = first_row + jnp.arange(row_total, dtype=jnp.int32)
    col_ids = jnp.arange(col_total, dtype=jnp.int32)
    slots = box_peaks.shape[2]
    alive = jnp.arange(slots, dtype=jnp.int32)[None, :] < box_count[:, None]
    row_gap = row_ids[None, :, None] - box_peaks[:, 0][:, None, :]
    col_gap = col_ids[None, :, None] - box_peaks[:, 1][:, None, :]
    distance = (row_gap * row_gap)[:, :, None, :] + (col_gap * col_gap)[:, None, :, :]
    member = (box_peaks[:, 2][:, :, None] == jnp.arange(classes, dtype=jnp.int32)) & alive[
        :, :, None
    ]
    gaussian = jnp.exp(-distance.astype(jnp.float32) / SPREAD_TWICE)
    heatmap = jnp.max(
        jnp.where(member[:, None, None], gaussian[..., None], jnp.float32(0.0)), axis=3
    )
    struck = jnp.any(member[:, None, None] & (distance == 0)[..., None], axis=3)
    return (heatmap, struck.astype(jnp.float32))


def rims(tensor):
    padded = extended(tensor, (("strip", 1),), 1)
    return jnp.pad(padded, ((0, 0), (0, 0), (1, 1), (0, 0)))


def rims_back(tensor):
    padded = extended(tensor, (("strip", 1),), 1)
    return jnp.pad(padded, ((0, 0), (0, 0), (1, 1), (0, 0)))


def conv_taps(padded, kernel, row_total, col_total):
    total = jnp.zeros((padded.shape[0], row_total, col_total, kernel.shape[3]), jnp.float32)
    for upward in range(3):
        for across in range(3):
            window = padded[:, upward : upward + row_total, across : across + col_total]
            total = total + jnp.einsum(
                "brwc,ch->brwh", window, kernel[upward, across], preferred_element_type=jnp.float32
            )
    return total


def kernel_taps(padded, grad_out):
    row_total, col_total = (grad_out.shape[1], grad_out.shape[2])
    pieces = []
    for upward in range(3):
        for across in range(3):
            window = padded[:, upward : upward + row_total, across : across + col_total]
            pieces.append(
                jnp.einsum("brwc,brwh->ch", window, grad_out, preferred_element_type=jnp.float32)
            )
    return jnp.stack(pieces).reshape((3, 3) + pieces[0].shape)


def flipped(kernel):
    return jnp.transpose(kernel, (0, 1, 3, 2))[::-1, ::-1]


def lift_points(features, depth_low, depth_bins):
    cam_logits = jnp.dot(features, depth_low, preferred_element_type=jnp.float32)
    depth = jax.nn.softmax(cam_logits[:, :depth_bins], axis=-1)
    context = cam_logits[:, depth_bins:]
    return (depth, context)


def padded_rows(features, ids, drop):
    flat_feat = features.reshape(-1, features.shape[-1])
    flat_ids = ids.reshape(-1, ids.shape[-1])
    count = flat_feat.shape[0]
    blocks = -(-count // pixel_block)
    extra = blocks * pixel_block - count
    flat_feat = jnp.pad(flat_feat, ((0, extra), (0, 0)))
    flat_ids = jnp.pad(flat_ids, ((0, extra), (0, 0)), constant_values=drop)
    return (
        flat_feat.reshape(blocks, pixel_block, flat_feat.shape[1]),
        flat_ids.reshape(blocks, pixel_block, flat_ids.shape[1]),
    )


def pool_blocks(features, ids, drop, depth_low, depth_bins):
    cam_width = depth_low.shape[1] - depth_bins
    feat_blocks, id_blocks = padded_rows(features, ids, drop)

    def pool_add_block(total, pair):
        feat, index = pair
        depth, context = lift_points(feat, depth_low, depth_bins)
        values = depth[:, :, None] * context[:, None, :]
        term = jax.ops.segment_sum(
            values.reshape(-1, cam_width), index.reshape(-1), num_segments=drop + 1
        )
        return (total + term, None)

    total, unused = lax.scan(
        pool_add_block, jnp.zeros((drop + 1, cam_width), jnp.float32), (feat_blocks, id_blocks)
    )
    return total[:drop]


def grad_blocks(features, ids, grid, drop, depth_low, depth_bins):
    cam_width = depth_low.shape[1] - depth_bins
    feat_blocks, id_blocks = padded_rows(features, ids, drop)

    def grad_add_block(total, pair):
        feat, index = pair
        depth, context = lift_points(feat, depth_low, depth_bins)
        picked = (
            jnp.take(grid, index.reshape(-1), axis=0)
            .reshape(index.shape + (cam_width,))
            .astype(jnp.float32)
        )
        grad_prob = jnp.einsum("pdc,pc->pd", picked, context, precision=lax.Precision.HIGHEST)
        grad_context = jnp.einsum("pdc,pd->pc", picked, depth, precision=lax.Precision.HIGHEST)
        grad_depth_logit = depth * (grad_prob - jnp.sum(grad_prob * depth, axis=-1, keepdims=True))
        grad_logits = jnp.concatenate([grad_depth_logit, grad_context], axis=-1).astype(
            jnp.bfloat16
        )
        return (
            total + jnp.einsum("pf,po->fo", feat, grad_logits, preferred_element_type=jnp.float32),
            None,
        )

    total, unused = lax.scan(
        grad_add_block, jnp.zeros(depth_low.shape, jnp.float32), (feat_blocks, id_blocks)
    )
    return total


def moments(values, cell_total, extra_term):
    total_sum, extra_term = lax.psum(
        (jnp.sum(values, axis=(0, 1, 2)), extra_term), ("batch", "strip")
    )
    center = total_sum / cell_total
    spread = (
        lax.psum(jnp.sum((values - center) ** 2, axis=(0, 1, 2)), ("batch", "strip")) / cell_total
    )
    return (center, lax.rsqrt(spread + EPS_NORM), extra_term)


def norm_backward(grad_norm, normed, gain, scale_inv, cell_total):
    grad_shift, grad_gain = lax.psum(
        (jnp.sum(grad_norm, axis=(0, 1, 2)), jnp.sum(grad_norm * normed, axis=(0, 1, 2))),
        ("batch", "strip"),
    )
    grad_in = (
        gain * scale_inv * (grad_norm - grad_shift / cell_total - normed * grad_gain / cell_total)
    )
    return (grad_in, grad_gain, grad_shift)


def silu_slope(value):
    sig = jax.nn.sigmoid(value)
    return sig * (1.0 + value * (1.0 - sig))


def adamw(weight, gradient, first, second, rate, step_value):
    first = 0.9 * first + 0.1 * gradient
    second = 0.999 * second + 0.001 * gradient * gradient
    fix_one = 1.0 - jnp.power(jnp.float32(0.9), step_value)
    fix_two = 1.0 - jnp.power(jnp.float32(0.999), step_value)
    update = first / fix_one / (jnp.sqrt(second / fix_two) + 1e-08) + 0.01 * weight
    return (weight - rate * update, first, second)


def squares(tensor):
    return jnp.sum(tensor * tensor)


def shards(
    camera_features,
    lidar_bev,
    pool_index,
    box_peaks,
    box_count,
    w_depth,
    m_depth,
    v_depth,
    w_join,
    m_join,
    v_join,
    w_res,
    m_res,
    v_res,
    w_head,
    m_head,
    v_head,
    norm_params,
    m_norm,
    v_norm,
    head_bias,
    m_bias,
    v_bias,
):
    samples, row_local, col_total, lidar_width = lidar_bev.shape
    strips = lax.axis_size("strip")
    row_total = row_local * strips
    cell_total = float(samples * lax.axis_size("batch") * row_total * col_total)
    depth_bins = pool_index.shape[2]
    classes = w_head.shape[1]
    owned = w_join.shape[3]
    cam_width = w_depth.shape[1] - depth_bins
    first_row = lax.axis_index("strip") * row_local
    join_full, res_full = (
        lax.all_gather(w_join.astype(jnp.bfloat16), "strip", axis=3, tiled=True),
        lax.all_gather(w_res.astype(jnp.bfloat16), "strip", axis=3, tiled=True),
    )
    depth_low = w_depth.astype(jnp.bfloat16)
    head_low = w_head.astype(jnp.bfloat16)
    grid_drop = samples * row_total * col_total
    offsets = (jnp.arange(samples, dtype=jnp.int32) * (row_total * col_total))[:, None, None]
    flat_ids = pool_index + offsets
    term = pool_blocks(camera_features, flat_ids, grid_drop, depth_low, depth_bins)
    pooled = lax.psum_scatter(
        term.reshape(samples, row_total, col_total, cam_width).astype(jnp.bfloat16),
        "strip",
        scatter_dimension=1,
        tiled=True,
    )
    joined = jnp.concatenate([pooled, lidar_bev], axis=-1)
    heatmap, struck = targets(box_peaks, box_count, first_row, row_local, col_total, classes)
    joined_pad = rims(joined)
    join_out = conv_taps(joined_pad, join_full, row_local, col_total)
    center_one, scale_one, positives = moments(join_out, cell_total, jnp.sum(struck))
    normed_one = (join_out - center_one) * scale_one
    pre_one = normed_one * norm_params[0] + norm_params[1]
    act_one = jax.nn.silu(pre_one).astype(jnp.bfloat16)
    act_pad = rims(act_one)
    res_out = conv_taps(act_pad, res_full, row_local, col_total)
    center_two, scale_two, unused_term = moments(res_out, cell_total, jnp.zeros((), jnp.float32))
    normed_two = (res_out - center_two) * scale_two
    summed = normed_two * norm_params[2] + norm_params[3] + act_one.astype(jnp.float32)
    hidden = jax.nn.silu(summed).astype(jnp.bfloat16)
    logits = (
        jnp.einsum("brwh,hk->brwk", hidden, head_low, preferred_element_type=jnp.float32)
        + head_bias
    )
    prob = jax.nn.sigmoid(logits)
    soft_neg = jax.nn.softplus(-logits)
    soft_pos = jax.nn.softplus(logits)
    weighting = (1.0 - heatmap) ** 4
    local_loss = jnp.sum(struck * (1.0 - prob) ** 2 * soft_neg + weighting * prob**2 * soft_pos)
    grad_pos = -2.0 * prob * (1.0 - prob) ** 2 * soft_neg - (1.0 - prob) ** 3
    grad_neg = 2.0 * prob**2 * (1.0 - prob) * soft_pos + prob**3
    grad_logits = ((struck * grad_pos + weighting * grad_neg) / positives).astype(jnp.bfloat16)
    grad_head = jnp.einsum("brwh,brwk->hk", hidden, grad_logits, preferred_element_type=jnp.float32)
    grad_bias = jnp.sum(grad_logits.astype(jnp.float32), axis=(0, 1, 2))
    grad_hidden = jnp.einsum(
        "brwk,hk->brwh", grad_logits, head_low, preferred_element_type=jnp.float32
    )
    grad_summed = grad_hidden * silu_slope(summed)
    grad_res_out, gain_two, shift_two = norm_backward(
        grad_summed, normed_two, norm_params[2], scale_two, cell_total
    )
    grad_res_low = grad_res_out.astype(jnp.bfloat16)
    grad_res = kernel_taps(act_pad, grad_res_low)
    grad_act = (
        conv_taps(rims_back(grad_res_low), flipped(res_full), row_local, col_total) + grad_summed
    )
    grad_pre = grad_act * silu_slope(pre_one)
    grad_join_out, gain_one, shift_one = norm_backward(
        grad_pre, normed_one, norm_params[0], scale_one, cell_total
    )
    grad_join_low = grad_join_out.astype(jnp.bfloat16)
    grad_join = kernel_taps(joined_pad, grad_join_low)
    grad_camera = conv_taps(
        rims_back(grad_join_low), flipped(join_full[:, :, :cam_width, :]), row_local, col_total
    ).astype(jnp.bfloat16)
    camera_grid = lax.all_gather(grad_camera, "strip", axis=1, tiled=True)
    whole_grid = jnp.concatenate(
        [camera_grid.reshape(grid_drop, cam_width), jnp.zeros((1, cam_width), jnp.bfloat16)], axis=0
    )
    grad_depth = grad_blocks(
        camera_features, flat_ids, whole_grid, grid_drop, depth_low, depth_bins
    )
    total_join, total_res, total_depth, total_head, total_bias, loss_sum = lax.psum(
        (grad_join, grad_res, grad_depth, grad_head, grad_bias, local_loss), ("batch", "strip")
    )
    norm_join = jnp.sqrt(squares(total_join))
    norm_res = jnp.sqrt(squares(total_res))
    start = lax.axis_index("strip") * owned
    total_join = lax.dynamic_slice_in_dim(total_join, start, owned, 3)
    total_res = lax.dynamic_slice_in_dim(total_res, start, owned, 3)
    grad_norm = jnp.stack([gain_one, shift_one, gain_two, shift_two])
    norms = [
        jnp.sqrt(squares(total_depth)),
        norm_join,
        norm_res,
        jnp.sqrt(squares(total_head)),
        jnp.sqrt(squares(grad_norm)),
        jnp.sqrt(squares(total_bias)),
    ]
    grads = [total_depth, total_join, total_res, total_head, grad_norm, total_bias]
    clipped = [
        gradient * (CLIP_NORM / jnp.maximum(norm_value, CLIP_NORM))
        for gradient, norm_value in zip(grads, norms)
    ]
    step_value = jnp.float32(STEP)
    rates = [
        0.5 * w_depth.shape[0] ** (-0.5),
        0.5 * (9 * w_join.shape[2]) ** (-0.5),
        0.5 * (9 * w_res.shape[2]) ** (-0.5),
        0.5 * w_head.shape[0] ** (-0.5),
        SMALL_RATE,
        SMALL_RATE,
    ]
    weights = [w_depth, w_join, w_res, w_head, norm_params, head_bias]
    firsts = [m_depth, m_join, m_res, m_head, m_norm, m_bias]
    seconds = [v_depth, v_join, v_res, v_head, v_norm, v_bias]
    result = [jnp.reshape(loss_sum / positives, (1,)), jnp.log(jnp.stack(norms))]
    for weight, gradient, first, second, rate in zip(weights, clipped, firsts, seconds, rates):
        result.extend(adamw(weight, gradient, first, second, rate, step_value))
    return tuple(result)


def solution(mesh):
    in_specs = (
        P("batch", "strip", None),
        P("batch", "strip", None, None),
        P("batch", "strip", None),
        P("batch", None, None),
        P("batch"),
        P(),
        P(),
        P(),
        P(None, None, None, "strip"),
        P(None, None, None, "strip"),
        P(None, None, None, "strip"),
        P(None, None, None, "strip"),
        P(None, None, None, "strip"),
        P(None, None, None, "strip"),
        P(),
        P(),
        P(),
        P(),
        P(),
        P(),
        P(),
        P(),
        P(),
    )
    out_specs = (
        P(),
        P(),
        P(),
        P(),
        P(),
        P(None, None, None, "strip"),
        P(None, None, None, "strip"),
        P(None, None, None, "strip"),
        P(None, None, None, "strip"),
        P(None, None, None, "strip"),
        P(None, None, None, "strip"),
        P(),
        P(),
        P(),
        P(),
        P(),
        P(),
        P(),
        P(),
        P(),
    )
    return jax.shard_map(shards, mesh=mesh, in_specs=in_specs, out_specs=out_specs, check_vma=False)
```

profile of v0, /device:TPU:0, one launch (start us, length us, event | category | flops | bytes accessed | tf_op | source)
XLA Modules:
  0.0 4064.7 jit_solution(15343610929213906113)
XLA Ops:
  15.5 1919.4 %while.21 = (s32[]{:T(128)}, f32[8641,80]{1,0:T(8,128)}, s32[5,512,118]{2,1,0:T(8,128)S(1)}, bf16[5,512,256]{2,1,0:T(8,128)(2,1)}, bf16[256,198]{1,0:T(8,128)(2,1)}, /*index=5*/s32[]{:T(128)}) while((s32[]{:T(128)}, f32[8641,80]{1,0:T(8,128)}, s32[5,512,118]{2,1,0:T(8,128)S(1)}, bf16[5,512,256]{2,1,0:T(8,128)(2,1)}, ...), condition=%wide.region_5.6_spmd, body=%wide.region_1.0_spmd.sunk | while | flops 61872128 | bytes 198015568 | solution.py:119
  25.0 20.2 mul.1109
  60.1 24.4 copy.209
  84.8 292.2 %scatter_fusion = f32[8641,80]{1,0:T(8,128)} fusion(f32[8641,80]{1,0:T(8,128)} %get-tuple-element.299, s32[60416]{0:T(1024)S(1)} %reshape.843, f32[60416,80]{1,0:T(8,128)} %copy.209), kind=kCustom, calls=%fused_computation.1.clone.1 | custom fusion | flops 4833280 | bytes 58241024 | tf_op jit(solution)/shard_map/while/body/eval_jaxpr/scatter-add | solution.py:114
  421.5 24.4 copy.209
  446.2 292.2 %scatter_fusion = f32[8641,80]{1,0:T(8,128)} fusion(f32[8641,80]{1,0:T(8,128)} %get-tuple-element.299, s32[60416]{0:T(1024)S(1)} %reshape.843, f32[60416,80]{1,0:T(8,128)} %copy.209), kind=kCustom, calls=%fused_computation.1.clone.1 | custom fusion | flops 4833280 | bytes 58241024 | tf_op jit(solution)/shard_map/while/body/eval_jaxpr/scatter-add | solution.py:114
  783.0 24.4 copy.209
  807.7 292.2 %scatter_fusion = f32[8641,80]{1,0:T(8,128)} fusion(f32[8641,80]{1,0:T(8,128)} %get-tuple-element.299, s32[60416]{0:T(1024)S(1)} %reshape.843, f32[60416,80]{1,0:T(8,128)} %copy.209), kind=kCustom, calls=%fused_computation.1.clone.1 | custom fusion | flops 4833280 | bytes 58241024 | tf_op jit(solution)/shard_map/while/body/eval_jaxpr/scatter-add | solution.py:114
  1144.4 24.4 copy.209
  1169.1 292.2 %scatter_fusion = f32[8641,80]{1,0:T(8,128)} fusion(f32[8641,80]{1,0:T(8,128)} %get-tuple-element.299, s32[60416]{0:T(1024)S(1)} %reshape.843, f32[60416,80]{1,0:T(8,128)} %copy.209), kind=kCustom, calls=%fused_computation.1.clone.1 | custom fusion | flops 4833280 | bytes 58241024 | tf_op jit(solution)/shard_map/while/body/eval_jaxpr/scatter-add | solution.py:114
  1505.9 24.4 copy.209
  1530.6 404.4 %scatter_fusion = f32[8641,80]{1,0:T(8,128)} fusion(f32[8641,80]{1,0:T(8,128)} %get-tuple-element.299, s32[60416]{0:T(1024)S(1)} %reshape.843, f32[60416,80]{1,0:T(8,128)} %copy.209), kind=kCustom, calls=%fused_computation.1.clone.1 | custom fusion | flops 4833280 | bytes 58241024 | tf_op jit(solution)/shard_map/while/body/eval_jaxpr/scatter-add | solution.py:114
  1988.1 21.3 all-gather.5.cloned.1.call-done
  2015.0 40.3 psum.105
  2055.5 38.9 psum.106
  2124.2 44.2 %psum.107 = f32[256]{0:T(256)S(1)} all-reduce(f32[256]{0:T(256)S(1)} %get-tuple-element.211), channel_id=1, replica_groups=mesh['batch'=4,'strip'=8] {'batch','strip'}, use_global_device_ids=true, to_apply=%region_12.13 | all-reduce | flops 256 | bytes 2048 | tf_op jit(solution)/shard_map/psum | solution.py:155
  2169.8 38.7 psum.108
  2213.6 41.5 %psum.110 = f32[]{:T(128)} all-reduce(f32[]{:T(128)} %get-tuple-element.132), channel_id=1, replica_groups=mesh['batch'=4,'strip'=8] {'batch','strip'}, use_global_device_ids=true, to_apply=%region_19.20 | all-reduce | flops 1 | bytes 8 | tf_op jit(solution)/shard_map/psum | solution.py:155
  2260.0 39.0 all-reduce.8
  2315.1 44.7 %all-reduce.7 = (f32[]{:T(128)}, f32[256]{0:T(256)S(1)}, f32[256]{0:T(256)S(1)}, f32[256,10]{0,1:T(8,128)}, f32[10]{0:T(128)}) all-reduce(f32[]{:T(128)} %get-tuple-element.133, f32[256]{0:T(256)S(1)} %get-tuple-element.127, f32[256]{0:T(256)S(1)} %get-tuple-element.126, ...), channel_id=1, replica_groups=mesh['batch'=4,'strip'=8] {'batch','strip'}, use_global_device_ids=true, to_apply=%region_17.18 | all-reduce | flops 3083 | bytes 24664 | tf_op jit(solution)/shard_map/psum | solution.py:300
  2408.9 1477.0 %while.22 = (s32[]{:T(128)}, f32[256,198]{0,1:T(8,128)}, bf16[5,512,256]{2,1,0:T(8,128)(2,1)}, bf16[256,198]{1,0:T(8,128)(2,1)}, s32[5,512,118]{2,1,0:T(8,128)},...) while((s32[]{:T(128)}, f32[256,198]{0,1:T(8,128)}, bf16[5,512,256]{2,1,0:T(8,128)(2,1)}, ...), condition=%wide.region_32.33_spmd.clone, body=%wide.region_28.32_spmd.clone.sunk | while | flops 144087552 | bytes 86831248 | solution.py:148
  2412.2 211.2 %gather_fusion = bf16[60416,80]{1,0:T(8,128)(2,1)} fusion(bf16[8641,80]{1,0:T(8,128)(2,1)S(1)} %get-tuple-element.331, s32[60416]{0:T(1024)S(1)} %broadcast_clamp_fusion.2), kind=kCustom, calls=%fused_computation.clone.clone.1 | custom fusion | bytes 19574784 | tf_op jit(solution)/shard_map/while/body/eval_jaxpr/jit(_take)/gather | solution.py:133
  2639.9 46.1 %gather.13 = bf16[512,118,80]{1,0,2:T(8,128)(2,1)} reshape(bf16[60416,80]{0,1:T(8,128)(2,1)} %copy.210) | data formatting | bytes 19333120 | tf_op jit(solution)/shard_map/while/body/eval_jaxpr/jit(_take)/gather | solution.py:133
  2707.6 211.2 %gather_fusion = bf16[60416,80]{1,0:T(8,128)(2,1)} fusion(bf16[8641,80]{1,0:T(8,128)(2,1)S(1)} %get-tuple-element.331, s32[60416]{0:T(1024)S(1)} %broadcast_clamp_fusion.2), kind=kCustom, calls=%fused_computation.clone.clone.1 | custom fusion | bytes 19574784 | tf_op jit(solution)/shard_map/while/body/eval_jaxpr/jit(_take)/gather | solution.py:133
  2935.2 46.1 %gather.13 = bf16[512,118,80]{1,0,2:T(8,128)(2,1)} reshape(bf16[60416,80]{0,1:T(8,128)(2,1)} %copy.210) | data formatting | bytes 19333120 | tf_op jit(solution)/shard_map/while/body/eval_jaxpr/jit(_take)/gather | solution.py:133
  3002.9 211.2 %gather_fusion = bf16[60416,80]{1,0:T(8,128)(2,1)} fusion(bf16[8641,80]{1,0:T(8,128)(2,1)S(1)} %get-tuple-element.331, s32[60416]{0:T(1024)S(1)} %broadcast_clamp_fusion.2), kind=kCustom, calls=%fused_computation.clone.clone.1 | custom fusion | bytes 19574784 | tf_op jit(solution)/shard_map/while/body/eval_jaxpr/jit(_take)/gather | solution.py:133
  3230.6 46.1 %gather.13 = bf16[512,118,80]{1,0,2:T(8,128)(2,1)} reshape(bf16[60416,80]{0,1:T(8,128)(2,1)} %copy.210) | data formatting | bytes 19333120 | tf_op jit(solution)/shard_map/while/body/eval_jaxpr/jit(_take)/gather | solution.py:133
  3298.3 211.2 %gather_fusion = bf16[60416,80]{1,0:T(8,128)(2,1)} fusion(bf16[8641,80]{1,0:T(8,128)(2,1)S(1)} %get-tuple-element.331, s32[60416]{0:T(1024)S(1)} %broadcast_clamp_fusion.2), kind=kCustom, calls=%fused_computation.clone.clone.1 | custom fusion | bytes 19574784 | tf_op jit(solution)/shard_map/while/body/eval_jaxpr/jit(_take)/gather | solution.py:133
  3525.9 46.1 %gather.13 = bf16[512,118,80]{1,0,2:T(8,128)(2,1)} reshape(bf16[60416,80]{0,1:T(8,128)(2,1)} %copy.210) | data formatting | bytes 19333120 | tf_op jit(solution)/shard_map/while/body/eval_jaxpr/jit(_take)/gather | solution.py:133
  3593.6 211.2 %gather_fusion = bf16[60416,80]{1,0:T(8,128)(2,1)} fusion(bf16[8641,80]{1,0:T(8,128)(2,1)S(1)} %get-tuple-element.331, s32[60416]{0:T(1024)S(1)} %broadcast_clamp_fusion.2), kind=kCustom, calls=%fused_computation.clone.clone.1 | custom fusion | bytes 19574784 | tf_op jit(solution)/shard_map/while/body/eval_jaxpr/jit(_take)/gather | solution.py:133
  3821.2 46.1 %gather.13 = bf16[512,118,80]{1,0,2:T(8,128)(2,1)} reshape(bf16[60416,80]{0,1:T(8,128)(2,1)} %copy.210) | data formatting | bytes 19333120 | tf_op jit(solution)/shard_map/while/body/eval_jaxpr/jit(_take)/gather | solution.py:133
  3893.8 147.4 %all-reduce.12.cloned.1.call-done = (f32[256,198]{0,1:T(8,128)}, f32[3,3,336,256]{2,3,1,0:T(8,128)}, f32[3,3,256,256]{2,3,1,0:T(8,128)}) async-done(((f32[256,198]{0,1:T(8,128)}, f32[3,3,336,256]{2,3,1,0:T(8,128)}, f32[3,3,256,256]{2,3,1,0:T(8,128)}), (f32[256,198]{0,1:T(8,128)}, f32[3,3,336,256]{2,3,1,0:T(8,128)}, f32[3,3,256,256]{2,3,1,0:T(8,128)})) %all-reduce.12.cloned.1.call-update) | async-done | bytes 5658640 | tf_op jit(solution)/shard_map/psum | solution.py:300
  (482 shorter events, 582.7 us)
Async XLA Ops:
  7.2 1974.7 %reduce-scatter.2.cloned.1.call-start = ((), (), s32[]{:S(2)}) async-start(), calls=%async_computation.1 | async-start | bytes 2543616 | tf_op jit(solution)/shard_map/reduce_scatter | solution.py:238
  1942.9 66.6 %all-gather.5.cloned.1.call-start = ((), (), s32[]{:S(2)}) async-start(), calls=%async_computation.2 | async-start | bytes 1990656 | tf_op jit(solution)/shard_map/all_gather | solution.py:229
  1944.6 172.2 %all-gather.7.cloned.1.call-start = ((), (), s32[]{:S(2)}) async-start(), calls=%async_computation.3 | async-start | bytes 1327104 | tf_op jit(solution)/shard_map/all_gather | solution.py:230
  1945.4 456.5 %all-gather.9.cloned.1.call-start = ((), (), s32[]{:S(2)}) async-start(), calls=%async_computation.4 | async-start | bytes 2211840 | tf_op jit(solution)/shard_map/all_gather | solution.py:293
  1945.6 36.3 copy-start.2
  1946.1 39.9 copy-start.60
  1982.9 3.7 collective-permute-start
  1984.2 3.3 collective-permute-start.1
  1986.6 108.5 %copy-start.55 = (f32[1,256]{1,0:T(1,128)}, f32[1,256]{1,0:T(1,128)S(1)}, u32[]{:S(2)}) copy-start(f32[1,256]{1,0:T(1,128)S(1)} %get-tuple-element.200) | copy-start | bytes 3076
  1986.6 108.5 %copy-start.68 = (f32[1,256]{1,0:T(1,128)}, f32[1,256]{1,0:T(1,128)S(1)}, u32[]{:S(2)}) copy-start(f32[1,256]{1,0:T(1,128)S(1)} %get-tuple-element.199) | copy-start | bytes 3076
  1986.6 25.0 copy-start.35
  1987.5 27.0 copy-start.33
  2055.3 40.1 copy-start.51
  2095.0 18.8 copy-start.53
  2096.2 17.6 slice-start
  2096.9 17.9 collective-permute-start.2
  2098.2 17.3 collective-permute-start.3
  2124.2 84.3 %copy-start.71 = (f32[1,256]{1,0:T(1,128)S(1)}, f32[1,256]{1,0:T(1,128)}, u32[]{:S(2)}) copy-start(f32[1,256]{1,0:T(1,128)} %get-tuple-element.198) | copy-start | bytes 3076
  2124.2 85.5 %copy-start.78 = (f32[1,256]{1,0:T(1,128)S(1)}, f32[1,256]{1,0:T(1,128)}, u32[]{:S(2)}) copy-start(f32[1,256]{1,0:T(1,128)} %get-tuple-element.201) | copy-start | bytes 3076
  2256.6 42.4 %copy-start.63 = (f32[256]{0:T(256)S(1)}, f32[256]{0:T(256)}, u32[]{:S(2)}) copy-start(f32[256]{0:T(256)} %copy-done.62) | copy-start | bytes 3076
  2256.6 42.4 %copy-start.77 = (f32[256]{0:T(256)S(1)}, f32[256]{0:T(256)}, u32[]{:S(2)}) copy-start(f32[256]{0:T(256)} %get-tuple-element.207) | copy-start | bytes 3076
  2300.9 11.4 copy-start.5
  2301.3 6.5 collective-permute-start.4
  2302.6 6.4 collective-permute-start.5
  2313.2 46.6 %copy-start.76 = (f32[256]{0:T(256)S(1)}, f32[256]{0:T(256)}, u32[]{:S(2)}) copy-start(f32[256]{0:T(256)} %get-tuple-element.205) | copy-start | bytes 3076
  2361.5 4.7 collective-permute-start.6
  2362.9 3.5 collective-permute-start.7
  2370.8 1670.4 %all-reduce.12.cloned.1.call-start = ((), (), s32[]{:S(2)}) async-start(), calls=%async_computation.5 | async-start | bytes 12206080 | tf_op jit(solution)/shard_map/psum | solution.py:300
  2694.0 8.5 copy-start.12
  2989.4 8.5 copy-start.12
  3284.7 8.5 copy-start.12
  3580.1 8.5 copy-start.12
  (78 other events, 215.2 us)
Sparse Core Ops, SparseCore 0:
  1943.0 38.8 reduce-scatter.1
  1984.1 25.3 all-gather.4
  2011.7 22.3 all-gather.6
  2370.9 30.9 all-gather.8
  3886.1 155.0 all-reduce.11
where the time goes:
time: 4080 us; the launch traced here: 4060 us
  other arithmetic  1800 us (44%)
  local copies, waits for them, and re-layouts  1690 us (41%)
  blocking collectives  287 us (7%)
  waiting for transfers between devices  204 us (5%)
  matrix products  53.1 us (1%)
    scatter-add x5, other arithmetic, pool_add_block(): jax.ops.segment_sum(values.reshape(-1, cam_width), index.reshape(-1), num...  1570 us
    gather x15, local copies, waits for them, and re-layouts, grad_add_block(): jnp.take(grid, index.reshape(-1), axis=0)  1370 us
    mul x20, local copies, waits for them, and re-layouts, pool_add_block(): values = depth[:, :, None] * context[:, None, :]  263 us
    psum x1, waiting for transfers between devices, shards(): lax.psum((grad_join, grad_res, grad_depth, grad_head, grad_bias, local_lo...  147 us
    psum x3, blocking collectives, moments(): lax.psum((jnp.sum(values, axis=(0, 1, 2)), extra_term), ('batch', 'strip'))  126 us
  transfers between devices with their start and end apart: 13, of which 6 were waited for; matrix products, arithmetic and copies ran while one was open for 2% of the time, Pallas kernels for 0%

commit v1 on v0

--- a/solution.py
+++ b/solution.py
@@ -1,6 +1,10 @@
+import functools
+
 import jax
 import jax.numpy as jnp
 from jax import lax
+from jax.experimental import pallas as pl
+from jax.experimental.pallas import tpu as pltpu
 from jax.sharding import PartitionSpec as P
 
 STEP = 5
@@ -10,7 +14,6 @@
 SPREAD_TWICE = 8.0
 SMALL_RATE = 0.25
 CLIP_NORM = 0.01
-pixel_block = 512
 
 
 def extended(shard, sides, width):
@@ -82,90 +85,244 @@
     return jnp.transpose(kernel, (0, 1, 3, 2))[::-1, ::-1]
 
 
-def lift_points(features, depth_low, depth_bins):
-    cam_logits = jnp.dot(features, depth_low, preferred_element_type=jnp.float32)
-    depth = jax.nn.softmax(cam_logits[:, :depth_bins], axis=-1)
-    context = cam_logits[:, depth_bins:]
-    return (depth, context)
-
-
-def padded_rows(features, ids, drop):
-    flat_feat = features.reshape(-1, features.shape[-1])
-    flat_ids = ids.reshape(-1, ids.shape[-1])
-    count = flat_feat.shape[0]
-    blocks = -(-count // pixel_block)
-    extra = blocks * pixel_block - count
-    flat_feat = jnp.pad(flat_feat, ((0, extra), (0, 0)))
-    flat_ids = jnp.pad(flat_ids, ((0, extra), (0, 0)), constant_values=drop)
-    return (
-        flat_feat.reshape(blocks, pixel_block, flat_feat.shape[1]),
-        flat_ids.reshape(blocks, pixel_block, flat_ids.shape[1]),
-    )
-
-
-def pool_blocks(features, ids, drop, depth_low, depth_bins):
-    cam_width = depth_low.shape[1] - depth_bins
-    feat_blocks, id_blocks = padded_rows(features, ids, drop)
-
-    def pool_add_block(total, pair):
-        feat, index = pair
-        depth, context = lift_points(feat, depth_low, depth_bins)
-        values = depth[:, :, None] * context[:, None, :]
-        term = jax.ops.segment_sum(
-            values.reshape(-1, cam_width), index.reshape(-1), num_segments=drop + 1
+LANES = 128
+BF = jnp.bfloat16
+F32 = jnp.float32
+
+
+def plan(pixels, strips, strip_cells):
+    per_strip = -(-strip_cells // LANES)
+    high = strips * per_strip
+    block = 176 if high <= 128 else 48
+    return dict(
+        per_strip=per_strip,
+        high=high,
+        high_pad=-(-high // 16) * 16,
+        offset=high // 2,
+        block=block,
+        stride=block + 4,
+        group=block // 4,
+        strip_cells=strip_cells,
+    )
+
+
+def split_cells(index, plan):
+    cell = index.astype(F32)
+    strip = jnp.floor((cell + 0.5) * (1.0 / plan["strip_cells"]))
+    rest = cell - strip * plan["strip_cells"]
+    part = jnp.floor((rest + 0.5) * (1.0 / LANES))
+    return strip * plan["per_strip"] + part - plan["offset"], rest - part * LANES
+
+
+def softmax_lanes(logits, bins):
+    lane = lax.broadcasted_iota(jnp.int32, logits.shape, 1)
+    logits = jnp.where(lane < bins, logits, -jnp.inf)
+    powers = jnp.exp(logits - jnp.max(logits, axis=1, keepdims=True))
+    return powers / jnp.sum(powers, axis=1, keepdims=True)
+
+
+def spread(ref, pixel):
+    return jnp.broadcast_to(ref[pl.ds(pixel, 1), :], (16, LANES)).astype(BF)
+
+
+def one_hot(row, value, rows, offset=0):
+    base = (lax.broadcasted_iota(jnp.int32, (rows, LANES), 0) - offset).astype(F32).astype(BF)
+    none = jnp.zeros((16, LANES), BF)
+    return [
+        jnp.where(base[k : k + 16] == row, value, none) for k in range(0, rows, 16)
+    ]
+
+
+def pool_kernel(feat_ref, index_ref, bins_ref, context_ref, pooled_ref, dense_ref, high_ref, low_ref, depth_ref, held, total, *, plan):
+    bins = index_ref.shape[1]
+    block, stride, high, high_pad = (plan[k] for k in ("block", "stride", "high", "high_pad"))
+    step = pl.program_id(0)
+
+    @pl.when(step == 0)
+    def _():
+        high_ref[...] = jnp.zeros_like(high_ref)
+        low_ref[...] = jnp.zeros_like(low_ref)
+        total[...] = jnp.zeros_like(total)
+
+    feat = feat_ref[...]
+    depth_ref[...] = softmax_lanes(jnp.dot(feat, bins_ref[...], preferred_element_type=F32), bins)
+    context = lax.dot_general(context_ref[...], feat, (((1,), (1,)), ((), ())), preferred_element_type=F32).astype(BF)
+    high_id, low_id = split_cells(index_ref[...], plan)
+    high_ref[:, :bins] = high_id
+    low_ref[:, :bins] = low_id
+    one = jnp.ones((16, LANES), BF)
+
+    def scatter(group, carry):
+        for k in range(0, plan["group"], 2):
+            first = group * plan["group"] + k
+            left, right = [], []
+            for j in range(2):
+                left += one_hot(spread(high_ref, first + j), spread(depth_ref, first + j), high_pad, plan["offset"])
+                right += one_hot(spread(low_ref, first + j), one, LANES)
+            tile = lax.dot_general(jnp.concatenate(left, 0), jnp.concatenate(right, 0), (((1,), (1,)), ((), ())), preferred_element_type=F32)
+            for j in range(2):
+                held[pl.ds(first + j, high, stride=stride), :] = tile[j * high_pad : j * high_pad + high, j * LANES : (j + 1) * LANES]
+        return carry
+
+    lax.fori_loop(0, block // plan["group"], scatter, 0)
+
+    def gather(k, carry):
+        parts = []
+        for j in range(2):
+            part = held[pl.ds((k * 2 + j) * stride, block), :].astype(BF)
+            dense_ref[k * 2 + j] = part
+            parts.append(part)
+        out = jnp.dot(context, jnp.concatenate(parts, 1), preferred_element_type=F32)
+        for j in range(2):
+            total[k * 2 + j] += out[:, j * LANES : (j + 1) * LANES]
+        return carry
+
+    lax.fori_loop(0, high // 2, gather, 0, unroll=2)
+
+    @pl.when(step == pl.num_programs(0) - 1)
+    def _():
+        pooled_ref[...] = total[...].astype(BF)
+
+
+def pool(features, index, bins_low, context_low, plan):
+    pixels, width = features.shape
+    bins = index.shape[1]
+    channels = context_low.shape[0]
+    block, high = plan["block"], plan["high"]
+    return pl.pallas_call(
+        functools.partial(pool_kernel, plan=plan),
+        grid=(pixels // block,),
+        in_specs=[
+            pl.BlockSpec((block, width), lambda i: (i, 0)),
+            pl.BlockSpec((block, bins), lambda i: (i, 0)),
+            pl.BlockSpec(bins_low.shape, lambda i: (0, 0)),
+            pl.BlockSpec(context_low.shape, lambda i: (0, 0)),
+        ],
+        out_specs=[
+            pl.BlockSpec((high, channels, LANES), lambda i: (0, 0, 0)),
+            pl.BlockSpec((high, block, LANES), lambda i: (0, i, 0)),
+        ],
+        out_shape=[
+            jax.ShapeDtypeStruct((high, channels, LANES), BF),
+            jax.ShapeDtypeStruct((high, pixels, LANES), BF),
+        ],
+        scratch_shapes=[pltpu.VMEM((block, LANES), F32)] * 3
+        + [
+            pltpu.VMEM((plan["high_pad"] * plan["stride"], LANES), F32),
+            pltpu.VMEM((high, channels, LANES), F32),
+        ],
+        compiler_params=pltpu.CompilerParams(vmem_limit_bytes=60 << 20),
+        name="pool",
+    )(features, index, bins_low, context_low)
+
+
+def unpool_kernel(feat_ref, index_ref, both_ref, dense_ref, grid_ref, grad_ref, high_ref, low_ref, pick_ref, held, *, plan):
+    bins = index_ref.shape[1]
+    channels = grid_ref.shape[2]
+    block, stride, high, high_pad = (plan[k] for k in ("block", "stride", "high", "high_pad"))
+    step = pl.program_id(0)
+
+    @pl.when(step == 0)
+    def _():
+        high_ref[...] = jnp.zeros_like(high_ref)
+        low_ref[...] = jnp.zeros_like(low_ref)
+        held[...] = jnp.zeros_like(held)
+        grad_ref[...] = jnp.zeros_like(grad_ref)
+
+    feat = feat_ref[...]
+    logits = jnp.dot(feat, both_ref[...], preferred_element_type=F32)
+    depth = softmax_lanes(logits[:, :LANES], bins)
+    context = logits[:, LANES : LANES + channels].astype(BF)
+    high_id, low_id = split_cells(index_ref[...], plan)
+    high_ref[:, :bins] = high_id
+    low_ref[:, :bins] = low_id
+
+    def project(k, carry):
+        grid = grid_ref[pl.ds(k * 2, 2)].reshape(2 * LANES, channels)
+        out = lax.dot_general(context, grid, (((1,), (1,)), ((), ())), preferred_element_type=F32)
+        for j in range(2):
+            held[pl.ds((k * 2 + j) * stride, block), :] = out[:, j * LANES : (j + 1) * LANES]
+        parts = [dense_ref[k * 2 + j] for j in range(2)]
+        return carry + jnp.dot(jnp.concatenate(parts, 1), grid, preferred_element_type=F32)
+
+    grad_context = lax.fori_loop(0, high // 2, project, jnp.zeros((block, channels), F32), unroll=2)
+    one = jnp.ones((16, LANES), BF)
+    rows = (lax.broadcasted_iota(jnp.int32, (high, LANES), 0) - plan["offset"]).astype(F32)
+
+    def collect(group, carry):
+        for k in range(0, plan["group"], 2):
+            first = group * plan["group"] + k
+            left, right = [], []
+            for j in range(2):
+                left.append(held[pl.ds(first + j, high_pad, stride=stride), :].astype(BF))
+                right.append(jnp.concatenate(one_hot(spread(low_ref, first + j), one, LANES), 0))
+            tile = jnp.dot(jnp.concatenate(left, 0), jnp.concatenate(right, 1), preferred_element_type=F32)
+            for j in range(2):
+                part = tile[j * high_pad : j * high_pad + high, j * LANES : (j + 1) * LANES]
+                kept = jnp.where(rows == high_ref[pl.ds(first + j, 1), :], part, 0.0)
+                pick_ref[pl.ds(first + j, 1), :] = jnp.sum(kept, axis=0, keepdims=True)
+        return carry
+
+    lax.fori_loop(0, block // plan["group"], collect, 0)
+    grad_prob = pick_ref[...]
+    grad_depth = depth * (grad_prob - jnp.sum(grad_prob * depth, axis=1, keepdims=True))
+    grad_low = jnp.concatenate(
+        [grad_depth, grad_context, jnp.zeros((block, LANES - channels), F32)], axis=1
+    ).astype(BF)
+    grad_ref[...] += lax.dot_general(feat, grad_low, (((0,), (0,)), ((), ())), preferred_element_type=F32)
+
+
+def unpool(features, index, both_low, dense, grid, plan):
+    pixels, width = features.shape
+    bins = index.shape[1]
+    channels = grid.shape[2]
+    block, high = plan["block"], plan["high"]
+    return pl.pallas_call(
+        functools.partial(unpool_kernel, plan=plan),
+        grid=(pixels // block,),
+        in_specs=[
+            pl.BlockSpec((block, width), lambda i: (i, 0)),
+            pl.BlockSpec((block, bins), lambda i: (i, 0)),
+            pl.BlockSpec(both_low.shape, lambda i: (0, 0)),
+            pl.BlockSpec((high, block, LANES), lambda i: (0, i, 0)),
+            pl.BlockSpec(grid.shape, lambda i: (0, 0, 0)),
+        ],
+        out_specs=pl.BlockSpec((width, 2 * LANES), lambda i: (0, 0)),
+        out_shape=jax.ShapeDtypeStruct((width, 2 * LANES), F32),
+        scratch_shapes=[pltpu.VMEM((block, LANES), F32)] * 3
+        + [pltpu.VMEM((plan["high_pad"] * plan["stride"], LANES), F32)],
+        compiler_params=pltpu.CompilerParams(vmem_limit_bytes=60 << 20),
+        name="unpool",
+    )(features, index, both_low, dense, grid)
+
+
+def everywhere(tensor):
+    axes = ("batch", "strip")
+    copies = jnp.broadcast_to(tensor[None], (lax.axis_size(axes),) + tensor.shape)
+    return lax.all_to_all(copies, axes, 0, 0)
+
+
+def summed_everywhere(tensor):
+    return jnp.sum(everywhere(tensor), axis=0)
+
+
+def moments(values, extra_term):
+    cells = values.shape[0] * values.shape[1] * values.shape[2]
+    center = jnp.sum(values, axis=(0, 1, 2)) / cells
+    spread_sum = jnp.sum((values - center) ** 2, axis=(0, 1, 2))
+    extra_row = jnp.full(center.shape, extra_term)
+    shared = everywhere(jnp.stack([center, spread_sum, extra_row]))
+    centers = shared[:, 0]
+    total = jnp.mean(centers, axis=0)
+    spread_mean = jnp.mean(shared[:, 1] / cells + (centers - total) ** 2, axis=0)
+    return (total, lax.rsqrt(spread_mean + EPS_NORM), jnp.sum(shared[:, 2, 0]))
+
+
+def norm_backward(grad_norm, normed, gain, scale_inv, cell_total):
+    grad_shift, grad_gain = summed_everywhere(
+        jnp.stack(
+            [jnp.sum(grad_norm, axis=(0, 1, 2)), jnp.sum(grad_norm * normed, axis=(0, 1, 2))]
         )
-        return (total + term, None)
-
-    total, unused = lax.scan(
-        pool_add_block, jnp.zeros((drop + 1, cam_width), jnp.float32), (feat_blocks, id_blocks)
-    )
-    return total[:drop]
-
-
-def grad_blocks(features, ids, grid, drop, depth_low, depth_bins):
-    cam_width = depth_low.shape[1] - depth_bins
-    feat_blocks, id_blocks = padded_rows(features, ids, drop)
-
-    def grad_add_block(total, pair):
-        feat, index = pair
-        depth, context = lift_points(feat, depth_low, depth_bins)
-        picked = (
-            jnp.take(grid, index.reshape(-1), axis=0)
-            .reshape(index.shape + (cam_width,))
-            .astype(jnp.float32)
-        )
-        grad_prob = jnp.einsum("pdc,pc->pd", picked, context, precision=lax.Precision.HIGHEST)
-        grad_context = jnp.einsum("pdc,pd->pc", picked, depth, precision=lax.Precision.HIGHEST)
-        grad_depth_logit = depth * (grad_prob - jnp.sum(grad_prob * depth, axis=-1, keepdims=True))
-        grad_logits = jnp.concatenate([grad_depth_logit, grad_context], axis=-1).astype(
-            jnp.bfloat16
-        )
-        return (
-            total + jnp.einsum("pf,po->fo", feat, grad_logits, preferred_element_type=jnp.float32),
-            None,
-        )
-
-    total, unused = lax.scan(
-        grad_add_block, jnp.zeros(depth_low.shape, jnp.float32), (feat_blocks, id_blocks)
-    )
-    return total
-
-
-def moments(values, cell_total, extra_term):
-    total_sum, extra_term = lax.psum(
-        (jnp.sum(values, axis=(0, 1, 2)), extra_term), ("batch", "strip")
-    )
-    center = total_sum / cell_total
-    spread = (
-        lax.psum(jnp.sum((values - center) ** 2, axis=(0, 1, 2)), ("batch", "strip")) / cell_total
-    )
-    return (center, lax.rsqrt(spread + EPS_NORM), extra_term)
-
-
-def norm_backward(grad_norm, normed, gain, scale_inv, cell_total):
-    grad_shift, grad_gain = lax.psum(
-        (jnp.sum(grad_norm, axis=(0, 1, 2)), jnp.sum(grad_norm * normed, axis=(0, 1, 2))),
-        ("batch", "strip"),
     )
     grad_in = (
         gain * scale_inv * (grad_norm - grad_shift / cell_total - normed * grad_gain / cell_total)
@@ -231,27 +388,25 @@
     )
     depth_low = w_depth.astype(jnp.bfloat16)
     head_low = w_head.astype(jnp.bfloat16)
-    grid_drop = samples * row_total * col_total
-    offsets = (jnp.arange(samples, dtype=jnp.int32) * (row_total * col_total))[:, None, None]
-    flat_ids = pool_index + offsets
-    term = pool_blocks(camera_features, flat_ids, grid_drop, depth_low, depth_bins)
-    pooled = lax.psum_scatter(
-        term.reshape(samples, row_total, col_total, cam_width).astype(jnp.bfloat16),
-        "strip",
-        scatter_dimension=1,
-        tiled=True,
-    )
+    strip_cells = row_local * col_total
+    layout = plan(camera_features.shape[1], strips, strip_cells)
+    bins_low = jnp.pad(depth_low[:, :depth_bins], ((0, 0), (0, LANES - depth_bins)))
+    context_low = depth_low[:, depth_bins:]
+    term, dense = pool(camera_features[0], pool_index[0], bins_low, context_low.T, layout)
+    pooled = lax.psum_scatter(term, "strip", scatter_dimension=0, tiled=True)
+    pooled = jnp.transpose(pooled, (0, 2, 1)).reshape(-1, cam_width)[:strip_cells]
+    pooled = pooled.reshape(samples, row_local, col_total, cam_width)
     joined = jnp.concatenate([pooled, lidar_bev], axis=-1)
     heatmap, struck = targets(box_peaks, box_count, first_row, row_local, col_total, classes)
     joined_pad = rims(joined)
     join_out = conv_taps(joined_pad, join_full, row_local, col_total)
-    center_one, scale_one, positives = moments(join_out, cell_total, jnp.sum(struck))
+    center_one, scale_one, positives = moments(join_out, jnp.sum(struck))
     normed_one = (join_out - center_one) * scale_one
     pre_one = normed_one * norm_params[0] + norm_params[1]
     act_one = jax.nn.silu(pre_one).astype(jnp.bfloat16)
     act_pad = rims(act_one)
     res_out = conv_taps(act_pad, res_full, row_local, col_total)
-    center_two, scale_two, unused_term = moments(res_out, cell_total, jnp.zeros((), jnp.float32))
+    center_two, scale_two, unused_term = moments(res_out, jnp.float32(0.0))
     normed_two = (res_out - center_two) * scale_two
     summed = normed_two * norm_params[2] + norm_params[3] + act_one.astype(jnp.float32)
     hidden = jax.nn.silu(summed).astype(jnp.bfloat16)
@@ -290,21 +445,42 @@
     grad_camera = conv_taps(
         rims_back(grad_join_low), flipped(join_full[:, :, :cam_width, :]), row_local, col_total
     ).astype(jnp.bfloat16)
-    camera_grid = lax.all_gather(grad_camera, "strip", axis=1, tiled=True)
-    whole_grid = jnp.concatenate(
-        [camera_grid.reshape(grid_drop, cam_width), jnp.zeros((1, cam_width), jnp.bfloat16)], axis=0
-    )
-    grad_depth = grad_blocks(
-        camera_features, flat_ids, whole_grid, grid_drop, depth_low, depth_bins
-    )
-    total_join, total_res, total_depth, total_head, total_bias, loss_sum = lax.psum(
-        (grad_join, grad_res, grad_depth, grad_head, grad_bias, local_loss), ("batch", "strip")
-    )
-    norm_join = jnp.sqrt(squares(total_join))
-    norm_res = jnp.sqrt(squares(total_res))
-    start = lax.axis_index("strip") * owned
-    total_join = lax.dynamic_slice_in_dim(total_join, start, owned, 3)
-    total_res = lax.dynamic_slice_in_dim(total_res, start, owned, 3)
+    cells = layout["per_strip"] * LANES
+    grad_cells = jnp.pad(
+        grad_camera.reshape(strip_cells, cam_width), ((0, cells - strip_cells), (0, 0))
+    ).reshape(layout["per_strip"], LANES, cam_width)
+    camera_grid = lax.all_gather(grad_cells, "strip", axis=0, tiled=True)
+    both_low = jnp.concatenate(
+        [bins_low, jnp.pad(context_low, ((0, 0), (0, LANES - cam_width)))], axis=1
+    )
+    grad_both = unpool(camera_features[0], pool_index[0], both_low, dense, camera_grid, layout)
+    grad_depth = jnp.concatenate(
+        [grad_both[:, :depth_bins], grad_both[:, LANES : LANES + cam_width]], axis=1
+    )
+    total_join, total_res = (
+        lax.psum(lax.psum_scatter(part, "strip", scatter_dimension=3, tiled=True), "batch")
+        for part in (grad_join, grad_res)
+    )
+    axes = ("batch", "strip")
+    devices = lax.axis_size(axes)
+    depth_share = lax.all_to_all(
+        grad_depth.reshape(devices, -1, grad_depth.shape[1]), axes, 0, 0
+    )
+    total_depth = everywhere(jnp.sum(depth_share, axis=0)).reshape(grad_depth.shape)
+    shares = lax.axis_size("batch")
+    small = jnp.concatenate(
+        [
+            grad_head.reshape(-1),
+            grad_bias,
+            jnp.stack([local_loss, squares(total_join) / shares, squares(total_res) / shares]),
+        ]
+    )
+    small = summed_everywhere(small)
+    total_head = small[: grad_head.size].reshape(grad_head.shape)
+    total_bias = small[grad_head.size : grad_head.size + classes]
+    loss_sum = small[-3]
+    norm_join = jnp.sqrt(small[-2])
+    norm_res = jnp.sqrt(small[-1])
     grad_norm = jnp.stack([gain_one, shift_one, gain_two, shift_two])
     norms = [
         jnp.sqrt(squares(total_depth)),

time: 4080 us -> 530 us (0.13)
  other arithmetic: 1800 us -> 62.5 us
  local copies, waits for them, and re-layouts: 1690 us -> 42.4 us
  blocking collectives: 287 us -> 38.5 us
  Pallas kernels: 0 us -> 170 us
  waiting for transfers between devices: 204 us -> 124 us
    scatter-add x5 -> x0, other arithmetic: 1570 us -> none  [pool_add_block(): jax.ops.segment_sum(values.reshape(-1, cam_width), index.reshape(-1), num...]
    gather x15 -> x0, local copies, waits for them, and re-layouts: 1370 us -> none  [grad_add_block(): jnp.take(grid, index.reshape(-1), axis=0)]
    psum x7 -> x0, blocking collectives: 287 us -> none  [the longest x3 126 us: moments(): lax.psum((jnp.sum(values, axis=(0, 1, 2)), extra_term), ('batch', 'strip'))]
    mul x20 -> x2, local copies, waits for them, and re-layouts: 263 us -> 0.21 us  [shards(): gradient * (CLIP_NORM / jnp.maximum(norm_value, CLIP_NORM))]
    pallas_call x0 -> x2, Pallas kernels: none -> 170 us  [the longest x1 94.8 us: unpool(): pl.pallas_call(functools.partial(unpool_kernel, plan=plan), grid=(pixels...]
    psum x1, waiting for transfers between devices: 147 us -> 0.02 us  [shards(): lax.psum(lax.psum_scatter(part, 'strip', scatter_dimension=3, tiled=True)...]
    mul x5 -> x1, other arithmetic: 74.4 us -> 0.01 us  [shards(): gradient * (CLIP_NORM / jnp.maximum(norm_value, CLIP_NORM))]
    reduce_scatter x1 -> x3, waiting for transfers between devices: 20.2 us -> 70.1 us  [the longest x2 37.1 us: shards(): lax.psum_scatter(part, 'strip', scatter_dimension=3, tiled=True)]
  transfers between devices with their start and end apart: 13 -> 19, of which waited for: 6 -> 9; matrix products, arithmetic and copies ran while one was open for 2% -> 18% of each run, Pallas kernels for 0% -> 18%
where the time goes in v1:
time: 530 us; the launch traced here: 521 us
  Pallas kernels  170 us (32%)
  waiting for transfers between devices  124 us (23%)
  other arithmetic  62.5 us (12%)
  local copies, waits for them, and re-layouts  42.4 us (8%)
  blocking collectives  38.5 us (7%)
  matrix products  30 us (6%)
  starting transfers between devices  28.9 us (5%)
  between operations  25.1 us (5%)
    pallas_call x1, Pallas kernels, unpool(): pl.pallas_call(functools.partial(unpool_kernel, plan=plan), grid=(pixels...  94.8 us
    pallas_call x1, Pallas kernels, pool(): pl.pallas_call(functools.partial(pool_kernel, plan=plan), grid=(pixels //...  75.2 us
    reduce_scatter x2, waiting for transfers between devices, shards(): lax.psum_scatter(part, 'strip', scatter_dimension=3, tiled=True)  37.1 us
    reduce_scatter x1, waiting for transfers between devices, shards(): pooled = lax.psum_scatter(term, 'strip', scatter_dimension=0, tiled=True)  33 us
    all_gather x1, waiting for transfers between devices, shards(): camera_grid = lax.all_gather(grad_cells, 'strip', axis=0, tiled=True)  24.5 us
    all_to_all x2, blocking collectives, everywhere(): return lax.all_to_all(copies, axes, 0, 0)  24.2 us
    all_to_all x4, waiting for transfers between devices, everywhere(): return lax.all_to_all(copies, axes, 0, 0)  20.8 us
    dot_general x36, matrix products, conv_taps(): jnp.einsum('brwc,ch->brwh', window, kernel[upward, across], preferred_ele...  18.1 us
  transfers between devices with their start and end apart: 19, of which 9 were waited for; matrix products, arithmetic and copies ran while one was open for 18% of the time, Pallas kernels for 18%

profile of v1, /device:TPU:0, one launch (start us, length us, event | category | flops | bytes accessed | tf_op | source)
XLA Modules:
  0.0 521.0 jit_solution(16426065914412302629)
XLA Ops:
  11.2 2.1 copy.351
  13.3 75.2 %pool.1 = (bf16[72,80,128]{2,1,0:T(8,128)(2,1)}, bf16[72,2112,128]{2,1,0:T(8,128)(2,1)}) custom-call(bf16[2112,256]{1,0:T(8,128)(2,1)} %bitcast.558, s32[2112,118]{1,0:T(8,128)} %bitcast.556, bf16[256,128]{1,0:T(8,128)(2,1)} %slice_select_fusion.bins_ref, bf16[80,256]{1,0:T(8,128)(2,1)} %copy.353.context_ref), custom_call_target="tpu_custom_call" | custom-call | tf_op jit(solution)/shard_map/pool/pallas_call | solution.py:192
  92.3 33.0 %reduce-scatter.4.cloned.1.call-done = bf16[9,80,128]{2,1,0:T(8,128)(2,1)} async-done(((bf16[72,80,128]{2,1,0:T(8,128)(2,1)}), bf16[9,80,128]{2,1,0:T(8,128)(2,1)}) %reduce-scatter.4.cloned.1.call-update) | async-done | bytes 184336 | tf_op jit(solution)/shard_map/reduce_scatter | solution.py:396
  129.6 14.3 %and_reduce_fusion = pred[6,180,10]{1,2,0:T(8,128)(4,1)S(1)} fusion(pred[6,180,150]{1,2,0:T(8,128)(4,1)S(1)} %add_compare_fusion, pred[150,10]{1,0:T(8,128)(4,1)S(1)} %fusion.91), kind=kLoop, calls=%fused_computation | loop fusion | flops 3229200 | bytes 174300 | tf_op jit(solution)/shard_map/reduce_or | solution.py:47
  145.9 6.1 %all-gather.4.cloned.1.call-done = bf16[3,3,336,256]{2,3,1,0:T(8,128)(2,1)} async-done(((bf16[3,3,336,32]{2,3,1,0:T(8,128)(2,1)}), bf16[3,3,336,256]{2,3,1,0:T(8,128)(2,1)}) %all-gather.4.cloned.1.call-update) | async-done | bytes 1548304 | tf_op jit(solution)/shard_map/all_gather | solution.py:386
  158.9 4.1 all-to-all-start
  163.7 10.6 %all-to-all-done = f32[32,3,256]{2,1,0:T(4,128)S(1)} async-done(((f32[32,3,256]{2,1,0:T(4,128)}), f32[32,3,256]{2,1,0:T(4,128)S(1)}, u32[]{:S(2)}, u32[]{:S(2)}) %all-to-all-start) | async-done | bytes 98336 | tf_op jit(solution)/shard_map/all_to_all | solution.py:302
  175.4 1.8 collective-permute-start.2
  189.3 5.6 %all-to-all-start.1 = ((f32[32,3,256]{2,1,0:T(4,128)}), f32[32,3,256]{2,1,0:T(4,128)}, u32[]{:S(2)}, u32[]{:S(2)}) async-start(f32[32,3,256]{2,1,0:T(4,128)} %broadcast_in_dim.31), calls=%async_computation.2 | async-start | bytes 262144 | tf_op jit(solution)/shard_map/all_to_all | solution.py:302
  194.9 17.1 %fusion = f32[6,180,10]{1,2,0:T(8,128)S(1)} fusion(pred[150,10]{1,0:T(8,128)(4,1)} %copy-done.45, f32[6,180,150]{1,2,0:T(8,128)} %fusion.33), kind=kLoop, calls=%fused_computation.2 | loop fusion | flops 3229200 | bytes 692700 | tf_op jit(solution)/shard_map/reduce_max | solution.py:44
  215.3 2.1 multiply_convert_fusion.2
  219.3 2.1 fusion.126
  221.5 13.0 %all_to_all.36 = f32[32,2,256]{2,1,0:T(2,128)S(1)} all-to-all(f32[32,2,256]{2,1,0:T(2,128)S(1)} %broadcast_in_dim.34), channel_id=1, replica_groups=mesh['batch'=4,'strip'=8] {'batch','strip'}, dimensions={0} | all-to-all | bytes 131072 | tf_op jit(solution)/shard_map/all_to_all | solution.py:302
  235.0 1.9 multiply_convert_fusion.1
  238.1 2.0 collective-permute-start.4
  247.1 3.1 copy.381
  255.9 2.8 fusion.125
  258.8 11.3 %all_to_all.37 = f32[32,2,256]{2,1,0:T(2,128)S(1)} all-to-all(f32[32,2,256]{2,1,0:T(2,128)S(1)} %broadcast_in_dim.35), channel_id=1, replica_groups=mesh['batch'=4,'strip'=8] {'batch','strip'}, dimensions={0} | all-to-all | bytes 131072 | tf_op jit(solution)/shard_map/all_to_all | solution.py:302
  279.2 5.0 copy.380
  284.3 2.7 collective-permute-start.6
  288.5 1.6 collective-permute-done.7
  294.7 37.1 %reduce-scatter.6.cloned.1.call-done = f32[3,3,336,32]{2,3,1,0:T(8,128)} async-done(((f32[3,3,336,256]{2,3,1,0:T(8,128)}), f32[3,3,336,32]{2,3,1,0:T(8,128)}) %reduce-scatter.6.cloned.1.call-update) | async-done | bytes 387088 | tf_op jit(solution)/shard_map/reduce_scatter | solution.py:461
  332.5 24.5 %all-gather.8.cloned.1.call-done = bf16[72,128,80]{1,2,0:T(8,128)(2,1)} async-done(((bf16[9,128,80]{1,2,0:T(8,128)(2,1)}), bf16[72,128,80]{1,2,0:T(8,128)(2,1)}) %all-gather.8.cloned.1.call-update) | async-done | bytes 1474576 | tf_op jit(solution)/shard_map/all_gather | solution.py:452
  357.0 3.9 copy.386.grid_ref
  360.8 94.8 %unpool.1 = f32[256,256]{1,0:T(8,128)} custom-call(bf16[2112,256]{1,0:T(8,128)(2,1)} %bitcast.559, s32[2112,118]{1,0:T(8,128)} %bitcast.557, bf16[256,256]{1,0:T(8,128)(2,1)} %fusion.76.both_ref, bf16[72,2112,128]{2,1,0:T(8,128)(2,1)} %get-tuple-element.23.dense_ref, bf16[72,128,80]{2,1,0:T(8,128)(2,1)} %copy.386.grid_ref), custom_call_target="tpu_custom_call" | custom-call | tf_op jit(solution)/shard_map/unpool/pallas_call | solution.py:280
  457.7 14.3 %all_to_all.38 = f32[32,8,198]{2,1,0:T(8,128)S(1)} all-to-all(f32[32,8,198]{2,1,0:T(8,128)S(1)} %maximum_bitcast_fusion), channel_id=1, replica_groups=mesh['batch'=4,'strip'=8] {'batch','strip'}, dimensions={0} | all-to-all | bytes 405504 | tf_op jit(solution)/shard_map/all_to_all | solution.py:466
  472.7 2.7 all-to-all-start.6
  476.1 1.7 multiply_reduce_fusion.5
  478.5 1.8 multiply_reduce_fusion.4
  481.7 4.2 all-to-all-done.6
  486.8 2.6 all-to-all-start.4
  495.8 6.0 %all-to-all-done.4 = f32[32,1,2573]{2,1,0:T(1,128)S(1)} async-done(((f32[32,1,2573]{2,1,0:T(1,128)}), f32[32,1,2573]{2,1,0:T(1,128)S(1)}, u32[]{:S(2)}, u32[]{:S(2)}) %all-to-all-start.4) | async-done | bytes 329376 | tf_op jit(solution)/shard_map/all_to_all | solution.py:302
  (354 shorter events, 85.1 us)
Async XLA Ops:
  7.2 118.0 %reduce-scatter.4.cloned.1.call-start = ((), (), s32[]{:S(2)}) async-start(), calls=%async_computation.10 | async-start | bytes 1658880 | tf_op jit(solution)/shard_map/reduce_scatter | solution.py:396
  88.5 63.5 %all-gather.4.cloned.1.call-start = ((), (), s32[]{:S(2)}) async-start(), calls=%async_computation.11 | async-start | bytes 1990656 | tf_op jit(solution)/shard_map/all_gather | solution.py:386
  90.2 91.0 %all-gather.6.cloned.1.call-start = ((), (), s32[]{:S(2)}) async-start(), calls=%async_computation.12 | async-start | bytes 1327104 | tf_op jit(solution)/shard_map/all_gather | solution.py:387
  91.0 35.8 %copy-start.2 = (bf16[1,6,180,256]{3,2,1,0:T(8,128)(2,1)S(1)}, bf16[1,6,180,256]{3,2,1,0:T(8,128)(2,1)}, u32[]{:S(2)}) copy-start(bf16[1,6,180,256]{3,2,1,0:T(8,128)(2,1)} %param.24) | copy-start | bytes 1658884
  92.0 37.5 %copy-start.45 = (pred[150,10]{1,0:T(8,128)(4,1)}, pred[150,10]{1,0:T(8,128)(4,1)S(1)}, u32[]{:S(2)}) copy-start(pred[150,10]{1,0:T(8,128)(4,1)S(1)} %fusion.91) | copy-start | bytes 4504
  127.0 18.3 %collective-permute-start = (bf16[1,1,180,336]{3,2,1,0:T(8,128)(2,1)S(1)}, bf16[1,1,180,336]{3,2,1,0:T(8,128)(2,1)S(1)}, u32[]{:S(2)}, u32[]{:S(2)}) collective-permute-start(bf16[1,1,180,336]{3,2,1,0:T(8,128)(2,1)S(1)} %get-tuple-element.192), channel_id=1, source_target_pairs={{0,1},{1,2},{2,3},{3,4},{4,5},{5,6},{6,7},{8,9},{9,10},{10,11},{11... | collective-permute-start | bytes 362888 | tf_op jit(solution)/shard_map/ppermute | solution.py:26
  128.3 17.0 %collective-permute-start.1 = (bf16[1,1,180,336]{3,2,1,0:T(8,128)(2,1)S(1)}, bf16[1,1,180,336]{3,2,1,0:T(8,128)(2,1)S(1)}, u32[]{:S(2)}, u32[]{:S(2)}) collective-permute-start(bf16[1,1,180,336]{3,2,1,0:T(8,128)(2,1)S(1)} %get-tuple-element.193), channel_id=1, source_target_pairs={{1,0},{2,1},{3,2},{4,3},{5,4},{6,5},{7,6},{9,8},{10,9},{11,10},{12... | collective-permute-start | bytes 362888 | tf_op jit(solution)/shard_map/ppermute | solution.py:27
  158.9 15.3 %all-to-all-start = ((f32[32,3,256]{2,1,0:T(4,128)}), f32[32,3,256]{2,1,0:T(4,128)S(1)}, u32[]{:S(2)}, u32[]{:S(2)}) async-start(f32[32,3,256]{2,1,0:T(4,128)} %broadcast_in_dim.30), calls=%async_computation.1 | async-start | bytes 262144 | tf_op jit(solution)/shard_map/all_to_all | solution.py:302
  163.7 21.1 %copy-start.59 = (f32[1,256]{1,0:T(1,128)}, f32[1,256]{1,0:T(1,128)S(1)}, u32[]{:S(2)}) copy-start(f32[1,256]{1,0:T(1,128)S(1)} %get-tuple-element.214) | copy-start | bytes 3076
  175.4 4.5 collective-permute-start.2
  177.2 3.2 collective-permute-start.3
  188.4 26.3 %copy-start.73 = (f32[1,256]{1,0:T(1,128)S(1)}, f32[1,256]{1,0:T(1,128)}, u32[]{:S(2)}) copy-start(f32[1,256]{1,0:T(1,128)} %get-tuple-element.212) | copy-start | bytes 3076
  189.3 24.2 %all-to-all-start.1 = ((f32[32,3,256]{2,1,0:T(4,128)}), f32[32,3,256]{2,1,0:T(4,128)}, u32[]{:S(2)}, u32[]{:S(2)}) async-start(f32[32,3,256]{2,1,0:T(4,128)} %broadcast_in_dim.31), calls=%async_computation.2 | async-start | bytes 262144 | tf_op jit(solution)/shard_map/all_to_all | solution.py:302
  194.9 99.8 %reduce-scatter.8.cloned.1.call-start = ((), (), s32[]{:S(2)}) async-start(), calls=%async_computation.14 | async-start | bytes 2654208 | tf_op jit(solution)/shard_map/reduce_scatter | solution.py:461
  238.1 12.4 %collective-permute-start.4 = (bf16[1,1,180,256]{3,2,1,0:T(8,128)(2,1)}, bf16[1,1,180,256]{3,2,1,0:T(8,128)(2,1)S(1)}, u32[]{:S(2)}, u32[]{:S(2)}) collective-permute-start(bf16[1,1,180,256]{3,2,1,0:T(8,128)(2,1)} %get-tuple-element.196), channel_id=1, source_target_pairs={{0,1},{1,2},{2,3},{3,4},{4,5},{5,6},{6,7},{8,9},{9,10},{10,11},{11... | collective-permute-start | bytes 276488 | tf_op jit(solution)/shard_map/ppermute | solution.py:26
  240.1 10.4 %collective-permute-start.5 = (bf16[1,1,180,256]{3,2,1,0:T(8,128)(2,1)}, bf16[1,1,180,256]{3,2,1,0:T(8,128)(2,1)}, u32[]{:S(2)}, u32[]{:S(2)}) collective-permute-start(bf16[1,1,180,256]{3,2,1,0:T(8,128)(2,1)} %get-tuple-element.197), channel_id=1, source_target_pairs={{1,0},{2,1},{3,2},{4,3},{5,4},{6,5},{7,6},{9,8},{10,9},{11,10},{12... | collective-permute-start | bytes 276488 | tf_op jit(solution)/shard_map/ppermute | solution.py:27
  250.2 81.5 %reduce-scatter.6.cloned.1.call-start = ((), (), s32[]{:S(2)}) async-start(), calls=%async_computation.13 | async-start | bytes 3981312 | tf_op jit(solution)/shard_map/reduce_scatter | solution.py:461
  284.2 72.8 %all-gather.8.cloned.1.call-start = ((), (), s32[]{:S(2)}) async-start(), calls=%async_computation.15 | async-start | bytes 1658880 | tf_op jit(solution)/shard_map/all_gather | solution.py:452
  284.3 4.2 collective-permute-start.6
  286.9 3.2 collective-permute-start.7
  293.2 38.5 %copy-start.26 = (bf16[256,128]{1,0:T(8,128)(2,1)S(1)}, bf16[256,128]{1,0:T(8,128)(2,1)}, u32[]{:S(2)}) copy-start(bf16[256,128]{1,0:T(8,128)(2,1)} %slice_select_fusion.bins_ref) | copy-start | bytes 196612
  293.2 38.5 %copy-start.40 = (bf16[256,80]{1,0:T(8,128)(2,1)S(1)}, bf16[256,80]{1,0:T(8,128)(2,1)}, u32[]{:S(2)}) copy-start(bf16[256,80]{1,0:T(8,128)(2,1)} %get-tuple-element.201) | copy-start | bytes 122884
  294.3 181.8 %all-reduce.9.cloned.1.call-start = ((), (), s32[]{:S(2)}) async-start(), calls=%async_computation.16 | async-start | bytes 1474560 | tf_op jit(solution)/shard_map/psum | solution.py:461
  456.5 18.9 %copy-start.17 = (bf16[6,180,256]{2,1,0:T(8,128)(2,1)S(1)}, bf16[6,180,256]{2,1,0:T(8,128)(2,1)}, u32[]{:S(2)}) copy-start(bf16[6,180,256]{2,1,0:T(8,128)(2,1)} %copy-done.16) | copy-start | bytes 1658884
  456.5 18.9 %copy-start.48 = (bf16[6,180,10]{1,2,0:T(8,128)(2,1)S(1)}, bf16[6,180,10]{1,2,0:T(8,128)(2,1)}, u32[]{:S(2)}) copy-start(bf16[6,180,10]{1,2,0:T(8,128)(2,1)} %copy-done.47) | copy-start | bytes 64804
  472.7 13.1 %all-to-all-start.6 = ((f32[32,8,198]{2,1,0:T(8,128)}), f32[32,8,198]{2,1,0:T(8,128)S(1)}, u32[]{:S(2)}, u32[]{:S(2)}) async-start(f32[32,8,198]{2,1,0:T(8,128)} %broadcast_in_dim.37), calls=%async_computation.9 | async-start | bytes 524288 | tf_op jit(solution)/shard_map/all_to_all | solution.py:302
  486.8 15.1 %all-to-all-start.4 = ((f32[32,1,2573]{2,1,0:T(1,128)}), f32[32,1,2573]{2,1,0:T(1,128)S(1)}, u32[]{:S(2)}, u32[]{:S(2)}) async-start(f32[32,1,2573]{2,1,0:T(1,128)} %broadcast_in_dim.36), calls=%async_computation.7 | async-start | bytes 688128 | tf_op jit(solution)/shard_map/all_to_all | solution.py:302
  493.4 16.2 %copy-start.63 = (f32[256,10]{0,1:T(8,128)S(1)}, f32[256,10]{0,1:T(8,128)}, u32[]{:S(2)}) copy-start(f32[256,10]{0,1:T(8,128)} %param.39) | copy-start | bytes 30724
  493.4 16.8 %copy-start.22 = (f32[3,3,256,32]{2,3,1,0:T(8,128)S(1)}, f32[3,3,256,32]{2,3,1,0:T(8,128)}, u32[]{:S(2)}) copy-start(f32[3,3,256,32]{2,3,1,0:T(8,128)} %param.34) | copy-start | bytes 884740
  493.4 16.8 %copy-start.23 = (f32[3,3,256,32]{2,3,1,0:T(8,128)S(1)}, f32[3,3,256,32]{2,3,1,0:T(8,128)}, u32[]{:S(2)}) copy-start(f32[3,3,256,32]{2,3,1,0:T(8,128)} %get-tuple-element.171) | copy-start | bytes 884740
  493.4 16.8 %copy-start.38 = (f32[3,3,256,32]{2,3,1,0:T(8,128)S(1)}, f32[3,3,256,32]{2,3,1,0:T(8,128)}, u32[]{:S(2)}) copy-start(f32[3,3,256,32]{2,3,1,0:T(8,128)} %param.36) | copy-start | bytes 884740
  493.4 16.8 %copy-start.39 = (f32[3,3,256,32]{2,3,1,0:T(8,128)S(1)}, f32[3,3,256,32]{2,3,1,0:T(8,128)}, u32[]{:S(2)}) copy-start(f32[3,3,256,32]{2,3,1,0:T(8,128)} %param.35) | copy-start | bytes 884740
  (75 other events, 370.7 us)
Sparse Core Ops, SparseCore 0:
  88.6 36.5 reduce-scatter.3
  127.4 24.5 all-gather.3
  154.2 24.5 all-gather.5
  250.3 36.2 reduce-scatter.7
  288.8 42.9 reduce-scatter.5
  333.9 23.0 all-gather.7
  360.4 47.8 all-reduce.8
